TPU v7x, 512 devices: a whole 4x8x8 slice. The times are simulated.
512 devices in a mesh: mode: 4 (over x), tm: 16 (over z, core), gz: 8 (over y).
Axes of the slice: x: 4, y: 8, z: 8, core: 2. Of those that a mesh axis runs over, the one named last changes fastest.
Arguments:
- vectors: bfloat16 [32, 2, 12, 262144], P('mode', None, None, ('tm', 'gz')), may hold values from -0.0024414062 to 0.0024414062
- sources: bfloat16 [12, 2, 12, 262144], P(None, None, None, ('tm', 'gz')), may hold values from -6 to 6
- eigenvalues: float32 [32], replicated, may hold values from 0.00159472 to 0.015947198
Outputs:
- guesses: float32 [12, 2, 12, 262144], P('mode', None, None, ('tm', 'gz'))
All inputs are finite; a program needn't handle non-finite values.
Results may differ from a plain program's by a relative error of at most 0.0035.
Values may be sent and summed in bfloat16 or wider, within the bound.
A program may use at most 64 MiB of HBM per device.

v0:
```python
import jax
import jax.numpy as jnp
from jax import lax
from jax.sharding import PartitionSpec as P


def contract_last(left, right):
    return lax.dot_general(
        left, right, (((1,), (1,)), ((), ())), preferred_element_type=jnp.float32
    )


def contract_first(left, right):
    return lax.dot_general(
        left, right, (((0,), (0,)), ((), ())), preferred_element_type=jnp.float32
    )


def split_parts(array):
    count = array.shape[0]
    return (array[:, 0].reshape(count, -1), array[:, 1].reshape(count, -1))


def coefficients(real_vec, imag_vec, real_src, imag_src):
    coef_real = contract_last(real_vec, real_src) + contract_last(imag_vec, imag_src)
    coef_imag = contract_last(real_vec, imag_src) - contract_last(imag_vec, real_src)
    return (coef_real, coef_imag)


def scaled(coef_real, coef_imag, eigen_block):
    scale_real = (coef_real / eigen_block[:, None]).astype(jnp.bfloat16)
    scale_imag = (coef_imag / eigen_block[:, None]).astype(jnp.bfloat16)
    return (scale_real, scale_imag)


def rebuild(scale_real, scale_imag, real_vec, imag_vec, comp_count):
    guess_real = contract_first(scale_real, real_vec) - contract_first(scale_imag, imag_vec)
    guess_imag = contract_first(scale_imag, real_vec) + contract_first(scale_real, imag_vec)
    return jnp.stack([guess_real, guess_imag], 1).reshape(guess_real.shape[0], 2, comp_count, -1)


def make_rows(scale_real, scale_imag, real_vec, imag_vec, comp_count):

    def guess_rows(start, count):
        return rebuild(scale_real, scale_imag, real_vec, imag_vec, comp_count)

    return guess_rows


def on_device(vectors, sources, eigenvalues):
    comp_count = vectors.shape[2]
    mode_count = vectors.shape[0]
    eigen_block = lax.dynamic_slice_in_dim(
        eigenvalues, lax.axis_index("mode") * mode_count, mode_count
    )
    real_vec, imag_vec = split_parts(vectors)
    real_src, imag_src = split_parts(sources)
    part_real, part_imag = coefficients(real_vec, imag_vec, real_src, imag_src)
    coef_real, coef_imag = lax.psum((part_real, part_imag), ("tm", "gz"))
    scale_real, scale_imag = scaled(coef_real, coef_imag, eigen_block)
    guess_rows = make_rows(scale_real, scale_imag, real_vec, imag_vec, comp_count)
    row_count = sources.shape[0] // lax.axis_size("mode")
    return lax.psum_scatter(
        guess_rows(jnp.int32(0), row_count * lax.axis_size("mode")),
        "mode",
        scatter_dimension=0,
        tiled=True,
    )


def solution(mesh):
    in_specs = (P("mode", None, None, ("tm", "gz")), P(None, None, None, ("tm", "gz")), P())
    out_specs = P("mode", None, None, ("tm", "gz"))
    return jax.shard_map(
        on_device, mesh=mesh, in_specs=in_specs, out_specs=out_specs, check_vma=False
    )
```

profile of v0, /device:TPU:1, one launch (start us, length us, event | category | flops | bytes accessed | tf_op | source)
XLA Modules:
  0.0 365.3 jit_solution(10132302313664176029)
XLA Ops:
  6.5 0.0 all-reduce.4.cloned.1.call-start
  6.5 3.0 fusion.9
  9.5 0.4 copy.20
  9.9 0.0 copy-done.1
  9.9 2.3 fusion.8
  12.3 0.4 copy.22
  12.7 0.8 convolution_bitcast_fusion.3
  13.5 0.8 convolution_bitcast_fusion.1
  14.2 0.8 fusion.1
  15.0 0.8 fusion
  15.8 254.8 %all-reduce.1 = (f32[8,12]{1,0:T(8,128)S(1)}, f32[8,12]{1,0:T(8,128)S(1)}) all-reduce(f32[8,12]{1,0:T(8,128)S(1)} %fusion, f32[8,12]{1,0:T(8,128)S(1)} %fusion.1), channel_id=1, replica_groups=mesh['mode'=4,'tm'=16,'gz'=8] {'tm','gz'}, use_global_device_ids=true, to_apply=%region_1.0 | all-reduce | flops 192 | bytes 1536 | tf_op jit(solution)/shard_map/psum | solution.py:59
  270.6 0.1 dynamic_slice.3
  270.7 0.5 fusion.6
  271.2 0.5 fusion.7
  271.6 1.6 convolution_subtract_fusion
  273.3 3.0 stack.9
  276.3 1.6 convolution_add_fusion
  277.9 2.0 stack.10
  279.9 0.3 pad_maximum_fusion
  280.2 3.2 copy.19
  283.5 0.0 all-reduce.4.cloned.1.call-update
  283.5 1.3 dynamic-slice
  285.4 71.1 %all-reduce.4.cloned.1.call-done = f32[12,2,12,2048]{3,1,2,0:T(2,128)} async-done(((f32[12,2,12,2048]{3,1,2,0:T(2,128)}), f32[12,2,12,2048]{3,1,2,0:T(2,128)}) %all-reduce.4.cloned.1.call-update) | async-done | bytes 2359312
  356.6 1.9 constant_dynamic-slice_fusion
  (5 shorter events, 0.0 us)
Async XLA Ops:
  6.5 350.0 %all-reduce.4.cloned.1.call-start = ((), (), s32[]{:S(2)}) async-start(), calls=%async_computation | async-start | bytes 4718592
  6.5 3.4 copy-start.1
  13.5 257.1 %copy-start.2 = (f32[32]{0:T(128)S(1)}, f32[32]{0:T(128)}, u32[]{:S(2)}) copy-start(f32[32]{0:T(128)} %param.5) | copy-start | bytes 388
  277.9 2.0 copy-start
Sparse Core Ops, SparseCore 0:
  283.6 72.8 all-reduce.3
where the time goes:
time: 366 us; the launch traced here: 365 us
  blocking collectives  255 us (70%)
  waiting for transfers between devices  71.2 us (19%)
  local copies, waits for them, and re-layouts  17.7 us (5%)
  between operations  14.1 us (4%)
  matrix products  7.28 us (2%)
    psum x1, blocking collectives, on_device(): coef_real, coef_imag = lax.psum((part_real, part_imag), ('tm', 'gz'))  255 us
    unnamed x2, waiting for transfers between devices  71.2 us
    another operation x3, local copies, waits for them, and re-layouts, rebuild(): jnp.stack([guess_real, guess_imag], 1)  8.22 us
  transfers between devices with their start and end apart: 1, of which 1 were waited for; matrix products, arithmetic and copies ran while one was open for 0% of the time, Pallas kernels for 0%

commit v1 on v0

v1 whole, which is shorter than its diff:
```python
import functools

import jax
import jax.numpy as jnp
from jax import lax
from jax.experimental import pallas as pl
from jax.experimental.pallas import tpu as pltpu
from jax.sharding import PartitionSpec as P

MESH = pl.DeviceIdType.MESH
F32, BF16 = jnp.float32, jnp.bfloat16
K, S, C, T = 8, 12, 12, 16
HALF = C // 2
VROWS, SROWS = K * 2 * T, S * 2 * T
OUT = 3


def iota(shape, dim):
    return lax.broadcasted_iota(jnp.int32, shape, dim)


def places():
    m, t, g = lax.axis_index("mode"), lax.axis_index("tm"), lax.axis_index("gz")
    near = m + 1 - 2 * lax.rem(m, 2)
    far = 3 - m
    return m, t, g, near, far


def plane_peers():
    m, t, g, _, _ = places()
    other = t + 1 - 2 * lax.rem(t, 2)
    peers = []
    for j in (4, 3, 5, 2, 6, 1, 7, 0):
        gz = lax.rem(g + j, 8)
        peers.append((m, other, gz))
        if j:
            peers.append((m, t, gz))
    return peers


def line_peers():
    m, t, g, near, far = places()
    peers = []
    for j in (4, 3, 5, 2, 6, 1, 7, 0):
        tm = lax.rem(t + 2 * j, 16)
        peers.append(((near, tm, g), 1))
        peers.append(((far, tm, g), 2))
        if j:
            peers.append(((m, tm, g), 0))
    return peers


def split3(x):
    high = x.astype(BF16)
    rest = x - high.astype(F32)
    mid = rest.astype(BF16)
    low = (rest - mid.astype(F32)).astype(BF16)
    return jnp.concatenate([high, mid, low], axis=0)


def same_tile():
    return (iota((32, VROWS), 0) // 2 == (iota((32, VROWS), 1) // 2) % T).astype(F32)


def partial_coefs(v, b):
    left = jnp.concatenate([b[:, c].reshape(SROWS, 128) for c in range(C)], axis=1)
    right = jnp.concatenate([v[:, c].reshape(VROWS, 128) for c in range(C)], axis=1)
    gram = lax.dot_general(left, right, (((1,), (1,)), ((), ())), preferred_element_type=F32)
    gram = gram.reshape(S, 32, VROWS) * same_tile()[None]
    x = gram.reshape(S, 4, 8, VROWS).sum(axis=1)
    x = x + pltpu.roll(x, 4, 1)
    x = x + pltpu.roll(x, 2, 1)
    sub = iota((8, VROWS), 0) // 2
    blocks = []
    for q in range(3):
        y = jnp.zeros((8, VROWS), F32)
        for i in range(4):
            y = jnp.where(sub == i, x[4 * q + i], y)
        blocks.append(y)
    y = split3(jnp.concatenate(blocks, axis=1))
    row, lane = iota((3 * VROWS, 128), 0), iota((3 * VROWS, 128), 1)
    pick = (lane == (row // VROWS) * 16 + ((row // 32) % K) * 2 + row % 2).astype(BF16)
    z = jnp.dot(y, pick, preferred_element_type=F32)
    return z[0:8] + z[8:16] + z[16:24]


def weights_of(sums, e_ref, modes, targets):
    sub, lane = iota((8, 128), 0), iota((8, 128), 1)
    rows = []
    for total, mode in zip(sums, modes):
        other = jnp.where(sub % 2 == 1, pltpu.roll(total, 1, 0), pltpu.roll(total, 7, 0))
        other = jnp.where(lane % 2 == 1, pltpu.roll(other, 1, 1), pltpu.roll(other, 127, 1))
        coef = total + jnp.where(sub % 2 == lane % 2, other, -other)
        eig = jnp.ones((8, 128), F32)
        for k in range(K):
            eig = jnp.where((lane // 2) % K == k, e_ref[mode * K + k], eig)
        rows.append((coef / eig).astype(BF16))
    small = jnp.concatenate(rows, axis=0)
    row, col = iota((128, 3 * VROWS), 0), iota((128, 3 * VROWS), 1)
    spread = (row == (col // VROWS) * 16 + ((col // 32) % K) * 2 + col % 2).astype(BF16)
    wide = jnp.dot(small, spread, preferred_element_type=F32)
    wide = jnp.concatenate(
        [
            jnp.concatenate([wide[8 * g : 8 * g + 8, q * VROWS : (q + 1) * VROWS] for q in range(3)], axis=0)
            for g in range(3)
        ],
        axis=1,
    ).astype(BF16)
    shape = (3 * 32 * OUT, 24)
    row, col = iota(shape, 0), iota(shape, 1)
    target = jnp.where(row < 32 * OUT, targets[0], jnp.where(row < 64 * OUT, targets[1], targets[2]))
    source = target * OUT + (row // 32) % OUT
    choose = (col == source * 2 + row % 2).astype(BF16)
    full = jnp.dot(choose, wide, preferred_element_type=F32)
    tile = same_tile()
    full = full.reshape(3 * OUT, 32, 3 * VROWS) * jnp.concatenate([tile] * 3, axis=1)[None]
    return full.reshape(3 * 32 * OUT, 3 * VROWS).astype(BF16)


def kernel(
    v_hbm, b_hbm, e_ref, o_ref,
    v, b, pair, first, slots1, second, slots2, send, recv,
    load_sem, pair_send, pair_recv, send1, recv1, send2, recv2, send3, recv3,
):
    m, t, g, near, far = places()
    core, z = lax.rem(t, 2), t // 2
    load_v = pltpu.make_async_copy(v_hbm, v, load_sem.at[0])
    load_b = pltpu.make_async_copy(b_hbm, b, load_sem.at[1])
    load_v.start()
    load_b.start()

    plane, line = plane_peers(), line_peers()
    barrier = pltpu.get_barrier_semaphore()
    for peer in plane + [p for p, _ in line]:
        pl.semaphore_signal(barrier, inc=1, device_id=peer, device_id_type=MESH)
    pl.semaphore_wait(barrier, len(plane) + len(line))

    load_v.wait()
    beside = ((near, t, g), (far, t, g))
    exchange = []
    for h in range(2):
        copy = pltpu.make_async_remote_copy(
            v.at[:, pl.ds(h * HALF, HALF)], pair.at[h], pair_send.at[h], pair_recv.at[h],
            device_id=beside[h], device_id_type=MESH,
        )
        copy.start()
        exchange.append(copy)
    load_b.wait()

    mine = partial_coefs(v, b)
    first[...] = mine
    own = g * 2 + core
    for peer in plane:
        pltpu.make_async_remote_copy(
            first, slots1.at[own], send1, recv1, device_id=peer, device_id_type=MESH
        ).start()
    slots1[own] = mine
    got = slots1.at[pl.ds(0, len(plane))]
    pltpu.make_async_copy(got, got, recv1).wait()
    total = slots1[...].sum(axis=0)

    second[...] = total
    for peer, group in line:
        pltpu.make_async_remote_copy(
            second, slots2.at[group * 8 + z], send2, recv2, device_id=peer, device_id_type=MESH
        ).start()
    slots2[z] = total
    got2 = slots2.at[pl.ds(0, len(line))]
    pltpu.make_async_copy(got2, got2, recv2).wait()
    sums = [slots2[8 * i : 8 * i + 8].sum(axis=0) for i in range(3)]

    w = weights_of(sums, e_ref, (m, near, far), (m, near, far))
    R = 32 * OUT
    sends = []
    for h in range(2):
        exchange[h].wait_recv()
        mate, dest = (1, 2) if h == 0 else (2, 1)
        left = jnp.concatenate(
            [
                jnp.concatenate([w[d * R : d * R + R, k * VROWS : (k + 1) * VROWS] for k in (0, mate)], axis=1)
                for d in (0, dest)
            ],
            axis=0,
        )
        right = jnp.concatenate(
            [
                jnp.concatenate([ref[:, c0 + c].reshape(VROWS, 128) for c in range(HALF)], axis=1)
                for ref, c0 in ((v, h * HALF), (pair.at[h], 0))
            ],
            axis=0,
        )
        out = jnp.dot(left, right, preferred_element_type=F32)
        for c in range(HALF):
            part = out[:, c * 128 : c * 128 + 128]
            o_ref[:, h * HALF + c] = part[:R].reshape(OUT, 32, 128)
            send[h, :, c] = part[R:].astype(BF16).reshape(OUT, 32, 128)
        copy = pltpu.make_async_remote_copy(
            send.at[h], recv.at[h], send3.at[h], recv3.at[h],
            device_id=beside[1 - h], device_id_type=MESH,
        )
        copy.start()
        sends.append(copy)
    for h in range(2):
        sends[h].wait_recv()
        o_ref[:, h * HALF : (h + 1) * HALF] += recv[h].astype(F32)

    for h in range(2):
        exchange[h].wait_send()
        sends[h].wait_send()
    pltpu.make_async_copy(got, got, send1).wait()
    pltpu.make_async_copy(got2, got2, send2).wait()


def on_device(vectors, sources, eigenvalues):
    def tiles(x):
        n = x.shape[0]
        return x.reshape(n, 2, C, T, 128).transpose(0, 2, 3, 1, 4).reshape(n, C, 2 * T, 128)

    dma = pltpu.SemaphoreType.DMA
    out = pl.pallas_call(
        kernel,
        out_shape=jax.ShapeDtypeStruct((OUT, C, 2 * T, 128), F32),
        in_specs=[
            pl.BlockSpec(memory_space=pltpu.HBM),
            pl.BlockSpec(memory_space=pltpu.HBM),
            pl.BlockSpec(memory_space=pltpu.SMEM),
        ],
        out_specs=pl.BlockSpec(memory_space=pltpu.VMEM),
        scratch_shapes=[
            pltpu.VMEM((K, C, 2 * T, 128), BF16),
            pltpu.VMEM((S, C, 2 * T, 128), BF16),
            pltpu.VMEM((2, K, HALF, 2 * T, 128), BF16),
            pltpu.VMEM((8, 128), F32),
            pltpu.VMEM((16, 8, 128), F32),
            pltpu.VMEM((8, 128), F32),
            pltpu.VMEM((24, 8, 128), F32),
            pltpu.VMEM((2, OUT, HALF, 2 * T, 128), BF16),
            pltpu.VMEM((2, OUT, HALF, 2 * T, 128), BF16),
            dma((2,)), dma((2,)), dma((2,)), dma, dma, dma, dma, dma((2,)), dma((2,)),
        ],
        compiler_params=pltpu.CompilerParams(
            collective_id=0, has_side_effects=True, vmem_limit_bytes=60 * 2**20
        ),
        name="deflate",
    )(tiles(vectors), tiles(sources), eigenvalues)
    return out.reshape(OUT, C, T, 2, 128).transpose(0, 3, 1, 2, 4).reshape(OUT, 2, C, T * 128)


def solution(mesh):
    in_specs = (P("mode", None, None, ("tm", "gz")), P(None, None, None, ("tm", "gz")), P())
    out_specs = P("mode", None, None, ("tm", "gz"))
    return jax.shard_map(
        on_device, mesh=mesh, in_specs=in_specs, out_specs=out_specs, check_vma=False
    )
```

time: 366 us -> 36.2 us (0.10)
  blocking collectives: 255 us -> 0 us
  waiting for transfers between devices: 71.2 us -> 0 us
  Pallas kernels: 0 us -> 34.1 us
  local copies, waits for them, and re-layouts: 17.7 us -> 1.92 us
  between operations: 14.1 us -> 0.01 us
  matrix products: 7.28 us -> 0 us
    psum x1 -> x0, blocking collectives: 255 us -> none  [on_device(): coef_real, coef_imag = lax.psum((part_real, part_imag), ('tm', 'gz'))]
    unnamed x2 -> x0, waiting for transfers between devices: 71.2 us -> none
    pallas_call x0 -> x1, Pallas kernels: none -> 34.1 us  [on_device(): pl.pallas_call(kernel, out_shape=jax.ShapeDtypeStruct((OUT, C, 2 * T, 128...]
    another operation x3 -> x0, local copies, waits for them, and re-layouts: 8.22 us -> none  [rebuild(): jnp.stack([guess_real, guess_imag], 1)]
    dot_general x8 -> x0, matrix products: 7.28 us -> none  [the longest x4 4.25 us: contract_first(): lax.dot_general(left, right, (((0,), (0,)), ((), ())), preferred_element_...]
    slice x2 -> x0, local copies, waits for them, and re-layouts: 5.3 us -> none  [split_parts(): return (array[:, 0].reshape(count, -1), array[:, 1].reshape(count, -1))]
  transfers between devices with their start and end apart: 1 -> 0, of which waited for: 1 -> 0; matrix products, arithmetic and copies ran while one was open for 0% -> 0% of each run, Pallas kernels for 0% -> 0%
where the time goes in v1:
time: 36.2 us; the launch traced here: 36 us
  Pallas kernels  34.1 us (94%)
  local copies, waits for them, and re-layouts  1.92 us (5%)
    pallas_call x1, Pallas kernels, on_device(): pl.pallas_call(kernel, out_shape=jax.ShapeDtypeStruct((OUT, C, 2 * T, 128...  34.1 us
    unnamed x1, local copies, waits for them, and re-layouts  1.92 us

profile of v1, /device:TPU:1, one launch (start us, length us, event | category | flops | bytes accessed | tf_op | source)
XLA Modules:
  0.0 36.0 jit_solution(8609114615355784710)
XLA Ops:
  0.0 34.1 %deflate.1 = f32[3,12,32,128]{3,2,1,0:T(8,128)} custom-call(bf16[8,12,32,128]{3,2,1,0:T(8,128)(2,1)} %bitcast.17, bf16[12,12,32,128]{3,2,1,0:T(8,128)(2,1)} %bitcast.16, f32[32]{0:T(128)} %e_ref.1), custom_call_target="tpu_custom_call" | custom-call | tf_op jit(solution)/shard_map/deflate/pallas_call | solution.py:220
  34.1 1.9 %copy.8 = f32[3,2,12,2048]{3,1,2,0:T(2,128)} copy(f32[3,2,12,2048]{3,1,2,0:T(2,128)} %bitcast.15) | data formatting | bytes 1179648

commit v2 on v1

v2 whole, which is shorter than its diff:
```python
import functools

import jax
import jax.numpy as jnp
from jax import lax
from jax.experimental import pallas as pl
from jax.experimental.pallas import tpu as pltpu
from jax.sharding import PartitionSpec as P

MESH = pl.DeviceIdType.MESH
F32, BF16 = jnp.float32, jnp.bfloat16
K, S, C, T = 8, 12, 12, 16
HALF = C // 2
VROWS, SROWS = K * 2 * T, S * 2 * T
OUT = 3
ROWS = 32 * OUT
Y_ORDER = (1, 0, 2, 3, 7, 6, 5, 4)


def iota(shape, dim):
    return lax.broadcasted_iota(jnp.int32, shape, dim)


def places():
    m, t, g = lax.axis_index("mode"), lax.axis_index("tm"), lax.axis_index("gz")
    near = m + 1 - 2 * lax.rem(m, 2)
    far = 3 - m
    return m, t, g, near, far


def plane_peers():
    m, t, _, _, _ = places()
    z = t // 2
    return [((m, 2 * z + core, gz), 0, True) for gz in Y_ORDER for core in range(2)]


def line_peers():
    m, t, g, near, far = places()
    core = lax.rem(t, 2)
    return [
        ((mode, 2 * z + core, g), group, group == 0)
        for z in range(8)
        for mode, group in ((far, 2), (near, 1), (m, 0))
    ]


def for_each(peers, act):
    _, t, g, _, _ = places()
    for place, group, can_be_self in peers:
        if can_be_self:
            pl.when(jnp.logical_or(place[1] != t, place[2] != g))(functools.partial(act, place, group))
        else:
            act(place, group)


def split3(x):
    high = x.astype(BF16)
    rest = x - high.astype(F32)
    mid = rest.astype(BF16)
    low = (rest - mid.astype(F32)).astype(BF16)
    return jnp.concatenate([high, mid, low], axis=0)


def same_tile():
    return (iota((32, VROWS), 0) // 2 == (iota((32, VROWS), 1) // 2) % T).astype(F32)


def partial_coefs(v, b):
    left = jnp.concatenate([b[:, c].reshape(SROWS, 128) for c in range(C)], axis=1)
    right = jnp.concatenate([v[:, c].reshape(VROWS, 128) for c in range(C)], axis=1)
    gram = lax.dot_general(left, right, (((1,), (1,)), ((), ())), preferred_element_type=F32)
    gram = gram.reshape(S, 32, VROWS) * same_tile()[None]
    x = gram.reshape(S, 4, 8, VROWS).sum(axis=1)
    x = x + pltpu.roll(x, 4, 1)
    x = x + pltpu.roll(x, 2, 1)
    sub = iota((8, VROWS), 0) // 2
    blocks = []
    for q in range(3):
        y = jnp.zeros((8, VROWS), F32)
        for i in range(4):
            y = jnp.where(sub == i, x[4 * q + i], y)
        blocks.append(y)
    y = split3(jnp.concatenate(blocks, axis=1))
    row, lane = iota((3 * VROWS, 128), 0), iota((3 * VROWS, 128), 1)
    pick = (lane == (row // VROWS) * 16 + ((row // 32) % K) * 2 + row % 2).astype(BF16)
    z = jnp.dot(y, pick, preferred_element_type=F32)
    return z[0:8] + z[8:16] + z[16:24]


def coefs_of(sums, e_ref, modes):
    sub, lane = iota((8, 128), 0), iota((8, 128), 1)
    rows = []
    for total, mode in zip(sums, modes):
        other = jnp.where(sub % 2 == 1, pltpu.roll(total, 1, 0), pltpu.roll(total, 7, 0))
        other = jnp.where(lane % 2 == 1, pltpu.roll(other, 1, 1), pltpu.roll(other, 127, 1))
        coef = total + jnp.where(sub % 2 == lane % 2, other, -other)
        eig = jnp.ones((8, 128), F32)
        for k in range(K):
            eig = jnp.where((lane // 2) % K == k, e_ref[mode * K + k], eig)
        rows.append((coef / eig).astype(BF16))
    small = jnp.concatenate(rows, axis=0)
    row, col = iota((128, 3 * VROWS), 0), iota((128, 3 * VROWS), 1)
    spread = (row == (col // VROWS) * 16 + ((col // 32) % K) * 2 + col % 2).astype(BF16)
    wide = jnp.dot(small, spread, preferred_element_type=F32)
    return jnp.concatenate(
        [
            jnp.concatenate([wide[8 * g : 8 * g + 8, q * VROWS : (q + 1) * VROWS] for q in range(3)], axis=0)
            for g in range(3)
        ],
        axis=1,
    ).astype(BF16)


def weights(wide, targets):
    n = len(targets)
    shape = (n * ROWS, 24)
    row, col = iota(shape, 0), iota(shape, 1)
    target = targets[0]
    for i in range(1, n):
        target = jnp.where(row < i * ROWS, target, targets[i])
    source = target * OUT + (row // 32) % OUT
    choose = (col == source * 2 + row % 2).astype(BF16)
    full = jnp.dot(choose, wide, preferred_element_type=F32)
    tile = jnp.concatenate([same_tile()] * (wide.shape[1] // VROWS), axis=1)
    return (full.reshape(n * OUT, 32, wide.shape[1]) * tile[None]).reshape(n * ROWS, wide.shape[1]).astype(BF16)


def kernel(
    v_hbm, b_hbm, e_hbm, o_ref,
    v, b, e, pair, first, slots1, second, slots2, send, recv,
    load_sem, pair_send, pair_recv, send1, recv1, send2, recv2, send3, recv3,
):
    m, t, g, near, far = places()
    core, z = lax.rem(t, 2), t // 2
    loads = [
        pltpu.make_async_copy(src, dst, load_sem.at[i])
        for i, (src, dst) in enumerate(((v_hbm, v), (b_hbm, b), (e_hbm, e)))
    ]
    for copy in loads:
        copy.start()

    plane, line = plane_peers(), line_peers()
    barrier = pltpu.get_barrier_semaphore()

    def greet(place, group):
        pl.semaphore_signal(barrier, inc=1, device_id=place, device_id_type=MESH)

    for_each(plane + line, greet)
    pl.semaphore_wait(barrier, len(plane) + len(line) - 2)

    loads[0].wait()
    beside = ((near, t, g), (far, t, g))
    exchange = []
    for h in range(2):
        copy = pltpu.make_async_remote_copy(
            v.at[:, pl.ds(h * HALF, HALF)], pair.at[h], pair_send.at[h], pair_recv.at[h],
            device_id=beside[h], device_id_type=MESH,
        )
        copy.start()
        exchange.append(copy)
    loads[1].wait()

    mine = partial_coefs(v, b)
    first[...] = mine
    own = g * 2 + core

    def post1(place, group):
        pltpu.make_async_remote_copy(
            first, slots1.at[own], send1, recv1, device_id=place, device_id_type=MESH
        ).start()

    for_each(plane, post1)
    slots1[own] = mine
    got = slots1.at[pl.ds(0, len(plane) - 1)]
    pltpu.make_async_copy(got, got, recv1).wait()
    total = slots1[...].sum(axis=0)

    second[...] = total

    def post2(place, group):
        pltpu.make_async_remote_copy(
            second, slots2.at[group * 8 + z], send2, recv2, device_id=place, device_id_type=MESH
        ).start()

    for_each(line, post2)
    slots2[z] = total
    got2 = slots2.at[pl.ds(0, len(line) - 1)]
    loads[2].wait()
    pltpu.make_async_copy(got2, got2, recv2).wait()
    sums = [slots2[8 * i : 8 * i + 8].sum(axis=0) for i in range(3)]

    wide = coefs_of(sums, e, (m, near, far))
    away = weights(wide, (far, near))

    def half(h, left):
        right = jnp.concatenate(
            [
                jnp.concatenate([ref[:, c0 + c].reshape(VROWS, 128) for c in range(HALF)], axis=1)
                for ref, c0 in ((v, h * HALF), (pair.at[h], 0))
            ],
            axis=0,
        )
        return jnp.dot(left, right, preferred_element_type=F32)

    def columns(w, h):
        mate = 1 + h
        return jnp.concatenate([w[:, :VROWS], w[:, mate * VROWS : (mate + 1) * VROWS]], axis=1)

    sends = []
    for h in range(2):
        exchange[h].wait_recv()
        out = half(h, columns(away[h * ROWS : (h + 1) * ROWS], h))
        for c in range(HALF):
            send[h, :, c] = out[:, c * 128 : c * 128 + 128].astype(BF16).reshape(OUT, 32, 128)
        copy = pltpu.make_async_remote_copy(
            send.at[h], recv.at[h], send3.at[h], recv3.at[h],
            device_id=beside[1 - h], device_id_type=MESH,
        )
        copy.start()
        sends.append(copy)
    home = weights(wide, (m,))
    for h in range(2):
        out = half(h, columns(home, h))
        for c in range(HALF):
            o_ref[:, h * HALF + c] = out[:, c * 128 : c * 128 + 128].reshape(OUT, 32, 128)

    for h in range(2):
        exchange[h].wait_send()
    pltpu.make_async_copy(got, got, send1).wait()
    pltpu.make_async_copy(got2, got2, send2).wait()
    for h in range(2):
        sends[h].wait_recv()
        o_ref[:, h * HALF : (h + 1) * HALF] += recv[h].astype(F32)
    for h in range(2):
        sends[h].wait_send()


def on_device(vectors, sources, eigenvalues):
    def tiles(x):
        n = x.shape[0]
        return x.reshape(n, 2, C, T, 128).transpose(0, 2, 3, 1, 4).reshape(n, C, 2 * T, 128)

    dma = pltpu.SemaphoreType.DMA
    out = pl.pallas_call(
        kernel,
        out_shape=pltpu.VMEM((OUT, C, 2 * T, 128), F32),
        in_specs=[
            pl.BlockSpec(memory_space=pltpu.HBM),
            pl.BlockSpec(memory_space=pltpu.HBM),
            pl.BlockSpec(memory_space=pltpu.HBM),
        ],
        out_specs=pl.BlockSpec(memory_space=pltpu.VMEM),
        scratch_shapes=[
            pltpu.VMEM((K, C, 2 * T, 128), BF16),
            pltpu.VMEM((S, C, 2 * T, 128), BF16),
            pltpu.SMEM((32,), F32),
            pltpu.VMEM((2, K, HALF, 2 * T, 128), BF16),
            pltpu.VMEM((8, 128), F32),
            pltpu.VMEM((16, 8, 128), F32),
            pltpu.VMEM((8, 128), F32),
            pltpu.VMEM((24, 8, 128), F32),
            pltpu.VMEM((2, OUT, HALF, 2 * T, 128), BF16),
            pltpu.VMEM((2, OUT, HALF, 2 * T, 128), BF16),
            dma((3,)), dma((2,)), dma((2,)), dma, dma, dma, dma, dma((2,)), dma((2,)),
        ],
        compiler_params=pltpu.CompilerParams(
            collective_id=0, has_side_effects=True, vmem_limit_bytes=60 * 2**20
        ),
        name="deflate",
    )(tiles(vectors), tiles(sources), eigenvalues)
    return out.reshape(OUT, C, T, 2, 128).transpose(0, 3, 1, 2, 4).reshape(OUT, 2, C, T * 128)


def solution(mesh):
    in_specs = (P("mode", None, None, ("tm", "gz")), P(None, None, None, ("tm", "gz")), P())
    out_specs = P("mode", None, None, ("tm", "gz"))
    return jax.shard_map(
        on_device, mesh=mesh, in_specs=in_specs, out_specs=out_specs, check_vma=False
    )
```

time: 36.2 us -> 33.5 us (0.925)
  Pallas kernels: 34.1 us -> 32.5 us
  local copies, waits for them, and re-layouts: 1.92 us -> 0.82 us
    pallas_call x1, Pallas kernels: 34.1 us -> 32.5 us  [on_device(): pl.pallas_call(kernel, out_shape=pltpu.VMEM((OUT, C, 2 * T, 128), F32), i...]
    unnamed x1, local copies, waits for them, and re-layouts: 1.92 us -> 0.82 us
where the time goes in v2:
time: 33.5 us; the launch traced here: 33.4 us
  Pallas kernels  32.5 us (97%)
  local copies, waits for them, and re-layouts  0.82 us (2%)
    pallas_call x1, Pallas kernels, on_device(): pl.pallas_call(kernel, out_shape=pltpu.VMEM((OUT, C, 2 * T, 128), F32), i...  32.5 us
    unnamed x1, local copies, waits for them, and re-layouts  0.82 us

profile of v2, /device:TPU:1, one launch (start us, length us, event | category | flops | bytes accessed | tf_op | source)
XLA Modules:
  0.0 33.4 jit_solution(2766616790046530165)
XLA Ops:
  0.0 32.5 %deflate.1 = f32[3,12,32,128]{3,2,1,0:T(8,128)S(1)} custom-call(bf16[8,12,32,128]{3,2,1,0:T(8,128)(2,1)} %bitcast.17, bf16[12,12,32,128]{3,2,1,0:T(8,128)(2,1)} %bitcast.16, f32[32]{0:T(128)} %e_hbm.1), custom_call_target="tpu_custom_call" | custom-call | tf_op jit(solution)/shard_map/deflate/pallas_call | solution.py:244
  32.5 0.8 %copy.8 = f32[3,2,12,2048]{3,1,2,0:T(2,128)} copy(f32[3,2,12,2048]{3,1,2,0:T(2,128)S(1)} %bitcast.15) | data formatting | bytes 1179648

commit v3 on v2

v3 whole, which is shorter than its diff:
```python
import functools

import jax
import jax.numpy as jnp
from jax import lax
from jax.experimental import pallas as pl
from jax.experimental.pallas import tpu as pltpu
from jax.sharding import PartitionSpec as P

MESH = pl.DeviceIdType.MESH
F32, BF16 = jnp.float32, jnp.bfloat16
K, S, C, T = 8, 12, 12, 16
HALF = C // 2
WIDTH = 2
VROWS, SROWS = K * 2 * T, S * 2 * T
OUT = 3
ROWS = 32 * OUT
Y_ORDER = (0, 1, 2, 3, 7, 6, 5, 4)


def iota(shape, dim):
    return lax.broadcasted_iota(jnp.int32, shape, dim)


def places():
    m, t, g = lax.axis_index("mode"), lax.axis_index("tm"), lax.axis_index("gz")
    near = m + 1 - 2 * lax.rem(m, 2)
    far = 3 - m
    return m, t, g, near, far


def plane_peers():
    m, t, g, _, _ = places()
    other = t + 1 - 2 * lax.rem(t, 2)
    at = 0
    for i, y in enumerate(Y_ORDER):
        at = jnp.where(g == y, i, at)
    peers = []
    for i in range(8):
        peers.append((m, other, Y_ORDER[i]))
        if i < 7:
            peers.append((m, t, jnp.where(i < at, Y_ORDER[i], Y_ORDER[i + 1])))
    return peers


def line_peers():
    m, t, g, near, far = places()
    z, core = t // 2, lax.rem(t, 2)
    peers = []
    for i in range(8):
        peers.append(((far, 2 * i + core, g), 2))
        peers.append(((near, 2 * i + core, g), 1))
        if i < 7:
            peers.append(((m, 2 * jnp.where(i < z, i, i + 1) + core, g), 0))
    return peers


def split3(x):
    high = x.astype(BF16)
    rest = x - high.astype(F32)
    mid = rest.astype(BF16)
    low = (rest - mid.astype(F32)).astype(BF16)
    return jnp.concatenate([high, mid, low], axis=0)


def same_tile():
    return (iota((32, VROWS), 0) // 2 == (iota((32, VROWS), 1) // 2) % T).astype(F32)


def partial_coefs(v, b, tile, pick):
    left = jnp.concatenate([b[:, c].reshape(SROWS, 128) for c in range(C)], axis=1)
    right = jnp.concatenate([v[:, c].reshape(VROWS, 128) for c in range(C)], axis=1)
    gram = lax.dot_general(left, right, (((1,), (1,)), ((), ())), preferred_element_type=F32)
    gram = gram.reshape(S, 32, VROWS) * tile[...][None]
    x = gram.reshape(S, 4, 8, VROWS).sum(axis=1)
    x = x + pltpu.roll(x, 4, 1)
    x = x + pltpu.roll(x, 2, 1)
    sub = iota((8, VROWS), 0) // 2
    blocks = []
    for q in range(3):
        y = jnp.zeros((8, VROWS), F32)
        for i in range(4):
            y = jnp.where(sub == i, x[4 * q + i], y)
        blocks.append(y)
    y = split3(jnp.concatenate(blocks, axis=1))
    z = jnp.dot(y, pick[...], preferred_element_type=F32)
    return z[0:8] + z[8:16] + z[16:24]


def tables1(tile, pick):
    tile[...] = same_tile()
    row, lane = iota((3 * VROWS, 128), 0), iota((3 * VROWS, 128), 1)
    pick[...] = (lane == (row // VROWS) * 16 + ((row // 32) % K) * 2 + row % 2).astype(BF16)


def tables2(spread, choose, targets):
    row, col = iota((128, 3 * VROWS), 0), iota((128, 3 * VROWS), 1)
    spread[...] = (row == (col // VROWS) * 16 + ((col // 32) % K) * 2 + col % 2).astype(BF16)
    row, col = iota((ROWS, 24), 0), iota((ROWS, 24), 1)
    for i, target in enumerate(targets):
        choose[i] = (col == (target * OUT + row // 32) * 2 + row % 2).astype(BF16)


def coefs_of(sums, eig, spread):
    sub, lane = iota((8, 128), 0), iota((8, 128), 1)
    rows = []
    for i, total in enumerate(sums):
        other = jnp.where(sub % 2 == 1, pltpu.roll(total, 1, 0), pltpu.roll(total, 7, 0))
        other = jnp.where(lane % 2 == 1, pltpu.roll(other, 1, 1), pltpu.roll(other, 127, 1))
        coef = total + jnp.where(sub % 2 == lane % 2, other, -other)
        rows.append((coef / eig[i]).astype(BF16))
    small = jnp.concatenate(rows, axis=0)
    wide = jnp.dot(small, spread[...], preferred_element_type=F32)
    return jnp.concatenate(
        [
            jnp.concatenate([wide[8 * g : 8 * g + 8, q * VROWS : (q + 1) * VROWS] for q in range(3)], axis=0)
            for g in range(3)
        ],
        axis=1,
    ).astype(BF16)


def weights(wide, choose, tile):
    n, blocks = choose.shape[0] // ROWS, wide.shape[1] // VROWS
    full = jnp.dot(choose, wide, preferred_element_type=F32)
    same = jnp.concatenate([tile[...]] * blocks, axis=1)
    return (full.reshape(n * OUT, 32, wide.shape[1]) * same[None]).reshape(choose.shape[0], wide.shape[1]).astype(BF16)


def kernel(
    v_hbm, b_hbm, e_hbm, o_ref,
    v, b, e, tile, pick, spread, choose, eig, pair, first, slots1, second, slots2, send, recv,
    load_sem, pair_send, pair_recv, send1, recv1, send2, recv2, send3, recv3,
):
    m, t, g, near, far = places()
    core, z = lax.rem(t, 2), t // 2
    loads = [
        pltpu.make_async_copy(src, dst, load_sem.at[i])
        for i, (src, dst) in enumerate(((v_hbm, v), (b_hbm, b), (e_hbm, e)))
    ]
    for copy in loads:
        copy.start()

    plane, line = plane_peers(), line_peers()
    barrier = pltpu.get_barrier_semaphore()
    for place in plane[::-1] + [p for p, _ in line]:
        pl.semaphore_signal(barrier, inc=1, device_id=place, device_id_type=MESH)
    tables1(tile, pick)
    loads[0].wait()
    loads[1].wait()
    mine = partial_coefs(v, b, tile, pick)
    first[...] = mine
    pl.semaphore_wait(barrier, len(plane) + len(line))

    own = g * 2 + core
    for place in plane:
        pltpu.make_async_remote_copy(
            first, slots1.at[own], send1, recv1, device_id=place, device_id_type=MESH
        ).start()
    beside = ((near, t, g), (far, t, g))
    exchange = []
    for h in range(2):
        copy = pltpu.make_async_remote_copy(
            v.at[:, pl.ds(h * HALF, HALF)], pair.at[h], pair_send.at[h], pair_recv.at[h],
            device_id=beside[h], device_id_type=MESH,
        )
        copy.start()
        exchange.append(copy)
    slots1[own] = mine
    tables2(spread, choose, (far, near, m))
    loads[2].wait()
    lane = iota((8, 128), 1)
    for i, mode in enumerate((m, near, far)):
        scale = jnp.ones((8, 128), F32)
        for k in range(K):
            scale = jnp.where((lane // 2) % K == k, e[mode * K + k], scale)
        eig[i] = scale
    got = slots1.at[pl.ds(0, len(plane))]
    pltpu.make_async_copy(got, got, recv1).wait()
    total = slots1[...].sum(axis=0)

    second[...] = total
    for place, group in line:
        pltpu.make_async_remote_copy(
            second, slots2.at[group * 8 + z], send2, recv2, device_id=place, device_id_type=MESH
        ).start()
    slots2[z] = total
    got2 = slots2.at[pl.ds(0, len(line))]
    pltpu.make_async_copy(got2, got2, recv2).wait()
    sums = [slots2[8 * i : 8 * i + 8].sum(axis=0) for i in range(3)]

    wide = coefs_of(sums, eig, spread)
    away = weights(wide, choose[0:2].reshape(2 * ROWS, 24), tile)

    def rows_of(left, start, h):
        right = jnp.concatenate(
            [
                jnp.concatenate([ref[:, c0 + c].reshape(VROWS, 128) for c in range(WIDTH)], axis=1)
                for ref, c0 in ((v, start), (pair.at[h], start - h * HALF))
            ],
            axis=0,
        )
        return jnp.dot(left, right, preferred_element_type=F32)

    def columns(w, h):
        mate = 1 + h
        return jnp.concatenate([w[:, :VROWS], w[:, mate * VROWS : (mate + 1) * VROWS]], axis=1)

    left = [columns(away[h * ROWS : (h + 1) * ROWS], h) for h in range(2)]
    sends = [None] * (C // WIDTH)
    for i in range(HALF // WIDTH):
        for h in range(2):
            if i == 0:
                exchange[h].wait_recv()
            start = h * HALF + i * WIDTH
            out = rows_of(left[h], start, h)
            for c in range(WIDTH):
                send[:, start + c] = out[:, c * 128 : c * 128 + 128].astype(BF16).reshape(OUT, 32, 128)
            part = pl.ds(start, WIDTH)
            n = start // WIDTH
            sends[n] = pltpu.make_async_remote_copy(
                send.at[:, part], recv.at[:, part], send3.at[n], recv3.at[n],
                device_id=beside[1 - h], device_id_type=MESH,
            )
            sends[n].start()
    home = weights(wide, choose[2], tile)
    for h in range(2):
        left = columns(home, h)
        for start in range(h * HALF, (h + 1) * HALF, WIDTH):
            out = rows_of(left, start, h)
            for c in range(WIDTH):
                o_ref[:, start + c] = out[:, c * 128 : c * 128 + 128].reshape(OUT, 32, 128)

    for h in range(2):
        exchange[h].wait_send()
    pltpu.make_async_copy(got, got, send1).wait()
    pltpu.make_async_copy(got2, got2, send2).wait()
    for i, copy in enumerate(sends):
        copy.wait_recv()
        part = slice(i * WIDTH, (i + 1) * WIDTH)
        o_ref[:, part] += recv[:, part].astype(F32)
    for copy in sends:
        copy.wait_send()


def on_device(vectors, sources, eigenvalues):
    def tiles(x):
        n = x.shape[0]
        return x.reshape(n, 2, C, T, 128).transpose(0, 2, 3, 1, 4).reshape(n, C, 2 * T, 128)

    dma = pltpu.SemaphoreType.DMA
    out = pl.pallas_call(
        kernel,
        out_shape=pltpu.VMEM((OUT, C, 2 * T, 128), F32),
        in_specs=[
            pl.BlockSpec(memory_space=pltpu.HBM),
            pl.BlockSpec(memory_space=pltpu.HBM),
            pl.BlockSpec(memory_space=pltpu.HBM),
        ],
        out_specs=pl.BlockSpec(memory_space=pltpu.VMEM),
        scratch_shapes=[
            pltpu.VMEM((K, C, 2 * T, 128), BF16),
            pltpu.VMEM((S, C, 2 * T, 128), BF16),
            pltpu.SMEM((32,), F32),
            pltpu.VMEM((32, VROWS), F32),
            pltpu.VMEM((3 * VROWS, 128), BF16),
            pltpu.VMEM((128, 3 * VROWS), BF16),
            pltpu.VMEM((3, ROWS, 24), BF16),
            pltpu.VMEM((3, 8, 128), F32),
            pltpu.VMEM((2, K, HALF, 2 * T, 128), BF16),
            pltpu.VMEM((8, 128), F32),
            pltpu.VMEM((16, 8, 128), F32),
            pltpu.VMEM((8, 128), F32),
            pltpu.VMEM((24, 8, 128), F32),
            pltpu.VMEM((OUT, C, 2 * T, 128), BF16),
            pltpu.VMEM((OUT, C, 2 * T, 128), BF16),
            dma((3,)), dma((2,)), dma((2,)), dma, dma, dma, dma, dma((C // WIDTH,)), dma((C // WIDTH,)),
        ],
        compiler_params=pltpu.CompilerParams(
            collective_id=0, has_side_effects=True, vmem_limit_bytes=60 * 2**20
        ),
        name="deflate",
    )(tiles(vectors), tiles(sources), eigenvalues)
    return out.reshape(OUT, C, T, 2, 128).transpose(0, 3, 1, 2, 4).reshape(OUT, 2, C, T * 128)


def solution(mesh):
    in_specs = (P("mode", None, None, ("tm", "gz")), P(None, None, None, ("tm", "gz")), P())
    out_specs = P("mode", None, None, ("tm", "gz"))
    return jax.shard_map(
        on_device, mesh=mesh, in_specs=in_specs, out_specs=out_specs, check_vma=False
    )
```

time: 33.5 us -> 31.6 us (0.943)
  Pallas kernels: 32.5 us -> 30.6 us
    pallas_call x1, Pallas kernels: 32.5 us -> 30.6 us  [on_device(): pl.pallas_call(kernel, out_shape=pltpu.VMEM((OUT, C, 2 * T, 128), F32), i...]
where the time goes in v3:
time: 31.6 us; the launch traced here: 31.5 us
  Pallas kernels  30.6 us (97%)
  local copies, waits for them, and re-layouts  0.82 us (3%)
    pallas_call x1, Pallas kernels, on_device(): pl.pallas_call(kernel, out_shape=pltpu.VMEM((OUT, C, 2 * T, 128), F32), i...  30.6 us
    unnamed x1, local copies, waits for them, and re-layouts  0.82 us

profile of v3, /device:TPU:1, one launch (start us, length us, event | category | flops | bytes accessed | tf_op | source)
XLA Modules:
  0.0 31.5 jit_solution(14837910772657342271)
XLA Ops:
  0.0 30.6 %deflate.1 = f32[3,12,32,128]{3,2,1,0:T(8,128)S(1)} custom-call(bf16[8,12,32,128]{3,2,1,0:T(8,128)(2,1)} %bitcast.17, bf16[12,12,32,128]{3,2,1,0:T(8,128)(2,1)} %bitcast.16, f32[32]{0:T(128)} %e_hbm.1), custom_call_target="tpu_custom_call" | custom-call | tf_op jit(solution)/shard_map/deflate/pallas_call | solution.py:252
  30.7 0.8 %copy.8 = f32[3,2,12,2048]{3,1,2,0:T(2,128)} copy(f32[3,2,12,2048]{3,1,2,0:T(2,128)S(1)} %bitcast.15) | data formatting | bytes 1179648

commit v4 on v3

--- a/solution.py
+++ b/solution.py
@@ -11,7 +11,7 @@
 F32, BF16 = jnp.float32, jnp.bfloat16
 K, S, C, T = 8, 12, 12, 16
 HALF = C // 2
-WIDTH = 2
+WIDTH = 3
 VROWS, SROWS = K * 2 * T, S * 2 * T
 OUT = 3
 ROWS = 32 * OUT
@@ -93,43 +93,54 @@
     pick[...] = (lane == (row // VROWS) * 16 + ((row // 32) % K) * 2 + row % 2).astype(BF16)
 
 
-def tables2(spread, choose, targets):
-    row, col = iota((128, 3 * VROWS), 0), iota((128, 3 * VROWS), 1)
-    spread[...] = (row == (col // VROWS) * 16 + ((col // 32) % K) * 2 + col % 2).astype(BF16)
-    row, col = iota((ROWS, 24), 0), iota((ROWS, 24), 1)
+def tables2(spread, row_of, targets):
+    row, col = iota((128, VROWS), 0), iota((128, VROWS), 1)
+    spread[...] = jnp.logical_and(row < 48, row % 16 == (col // 32) * 2 + col % 2).astype(BF16)
+    sub, lane = iota((8, 128), 0), iota((8, 128), 1)
     for i, target in enumerate(targets):
-        choose[i] = (col == (target * OUT + row // 32) * 2 + row % 2).astype(BF16)
-
-
-def coefs_of(sums, eig, spread):
+        for j in range(OUT):
+            source = target * OUT + j
+            here = jnp.logical_and(sub // 2 == source % 4, lane // 16 == source // 4)
+            row_of[i * OUT + j] = here.astype(F32)
+
+
+def coefs_of(sums, inverse):
     sub, lane = iota((8, 128), 0), iota((8, 128), 1)
-    rows = []
+    blocks = []
     for i, total in enumerate(sums):
         other = jnp.where(sub % 2 == 1, pltpu.roll(total, 1, 0), pltpu.roll(total, 7, 0))
         other = jnp.where(lane % 2 == 1, pltpu.roll(other, 1, 1), pltpu.roll(other, 127, 1))
         coef = total + jnp.where(sub % 2 == lane % 2, other, -other)
-        rows.append((coef / eig[i]).astype(BF16))
-    small = jnp.concatenate(rows, axis=0)
-    wide = jnp.dot(small, spread[...], preferred_element_type=F32)
-    return jnp.concatenate(
-        [
-            jnp.concatenate([wide[8 * g : 8 * g + 8, q * VROWS : (q + 1) * VROWS] for q in range(3)], axis=0)
-            for g in range(3)
-        ],
-        axis=1,
-    ).astype(BF16)
-
-
-def weights(wide, choose, tile):
-    n, blocks = choose.shape[0] // ROWS, wide.shape[1] // VROWS
-    full = jnp.dot(choose, wide, preferred_element_type=F32)
-    same = jnp.concatenate([tile[...]] * blocks, axis=1)
-    return (full.reshape(n * OUT, 32, wide.shape[1]) * same[None]).reshape(choose.shape[0], wide.shape[1]).astype(BF16)
+        blocks.append((coef * inverse[i]).astype(BF16).astype(F32))
+    return blocks
+
+
+def weights(blocks, row_of, wanted, spread, tile):
+    small = []
+    for target, use in wanted:
+        for j in range(OUT):
+            for g in use:
+                x = blocks[g] * row_of[target * OUT + j]
+                x = x + pltpu.roll(x, 4, 0)
+                small.append(x + pltpu.roll(x, 2, 0))
+    wide = jnp.dot(jnp.concatenate(small, axis=0).astype(BF16), spread[...], preferred_element_type=F32)
+    result, at = [], 0
+    same = tile[...]
+    for target, use in wanted:
+        rows = []
+        for j in range(OUT):
+            row = []
+            for g in use:
+                row.append(jnp.concatenate([wide[at : at + 8]] * 4, axis=0) * same)
+                at += 8
+            rows.append(jnp.concatenate(row, axis=1))
+        result.append(jnp.concatenate(rows, axis=0).astype(BF16))
+    return result
 
 
 def kernel(
     v_hbm, b_hbm, e_hbm, o_ref,
-    v, b, e, tile, pick, spread, choose, eig, pair, first, slots1, second, slots2, send, recv,
+    v, b, e, tile, pick, spread, row_of, inverse, pair, first, slots1, second, slots2, send, recv,
     load_sem, pair_send, pair_recv, send1, recv1, send2, recv2, send3, recv3,
 ):
     m, t, g, near, far = places()
@@ -167,14 +178,14 @@
         copy.start()
         exchange.append(copy)
     slots1[own] = mine
-    tables2(spread, choose, (far, near, m))
+    tables2(spread, row_of, (far, near, m))
     loads[2].wait()
     lane = iota((8, 128), 1)
     for i, mode in enumerate((m, near, far)):
         scale = jnp.ones((8, 128), F32)
         for k in range(K):
             scale = jnp.where((lane // 2) % K == k, e[mode * K + k], scale)
-        eig[i] = scale
+        inverse[i] = 1.0 / scale
     got = slots1.at[pl.ds(0, len(plane))]
     pltpu.make_async_copy(got, got, recv1).wait()
     total = slots1[...].sum(axis=0)
@@ -189,8 +200,8 @@
     pltpu.make_async_copy(got2, got2, recv2).wait()
     sums = [slots2[8 * i : 8 * i + 8].sum(axis=0) for i in range(3)]
 
-    wide = coefs_of(sums, eig, spread)
-    away = weights(wide, choose[0:2].reshape(2 * ROWS, 24), tile)
+    blocks = coefs_of(sums, inverse)
+    left = weights(blocks, row_of, ((0, (0, 1)), (1, (0, 2))), spread, tile)
 
     def rows_of(left, start, h):
         right = jnp.concatenate(
@@ -202,11 +213,6 @@
         )
         return jnp.dot(left, right, preferred_element_type=F32)
 
-    def columns(w, h):
-        mate = 1 + h
-        return jnp.concatenate([w[:, :VROWS], w[:, mate * VROWS : (mate + 1) * VROWS]], axis=1)
-
-    left = [columns(away[h * ROWS : (h + 1) * ROWS], h) for h in range(2)]
     sends = [None] * (C // WIDTH)
     for i in range(HALF // WIDTH):
         for h in range(2):
@@ -223,11 +229,10 @@
                 device_id=beside[1 - h], device_id_type=MESH,
             )
             sends[n].start()
-    home = weights(wide, choose[2], tile)
+    home = weights(blocks, row_of, ((2, (0, 1)), (2, (0, 2))), spread, tile)
     for h in range(2):
-        left = columns(home, h)
         for start in range(h * HALF, (h + 1) * HALF, WIDTH):
-            out = rows_of(left, start, h)
+            out = rows_of(home[h], start, h)
             for c in range(WIDTH):
                 o_ref[:, start + c] = out[:, c * 128 : c * 128 + 128].reshape(OUT, 32, 128)
 
@@ -264,8 +269,8 @@
             pltpu.SMEM((32,), F32),
             pltpu.VMEM((32, VROWS), F32),
             pltpu.VMEM((3 * VROWS, 128), BF16),
-            pltpu.VMEM((128, 3 * VROWS), BF16),
-            pltpu.VMEM((3, ROWS, 24), BF16),
+            pltpu.VMEM((128, VROWS), BF16),
+            pltpu.VMEM((3 * OUT, 8, 128), F32),
             pltpu.VMEM((3, 8, 128), F32),
             pltpu.VMEM((2, K, HALF, 2 * T, 128), BF16),
             pltpu.VMEM((8, 128), F32),

time: 31.6 us -> 31.3 us (level)
    pallas_call x1, Pallas kernels: 30.6 us -> 30.3 us  [on_device(): pl.pallas_call(kernel, out_shape=pltpu.VMEM((OUT, C, 2 * T, 128), F32), i...]
where the time goes in v4:
time: 31.3 us; the launch traced here: 31.1 us
  Pallas kernels  30.3 us (97%)
  local copies, waits for them, and re-layouts  0.82 us (3%)
    pallas_call x1, Pallas kernels, on_device(): pl.pallas_call(kernel, out_shape=pltpu.VMEM((OUT, C, 2 * T, 128), F32), i...  30.3 us
    unnamed x1, local copies, waits for them, and re-layouts  0.82 us

profile of v4, /device:TPU:1, one launch (start us, length us, event | category | flops | bytes accessed | tf_op | source)
XLA Modules:
  0.0 31.1 jit_solution(13583540719542756214)
XLA Ops:
  0.0 30.3 %deflate.1 = f32[3,12,32,128]{3,2,1,0:T(8,128)S(1)} custom-call(bf16[8,12,32,128]{3,2,1,0:T(8,128)(2,1)} %bitcast.17, bf16[12,12,32,128]{3,2,1,0:T(8,128)(2,1)} %bitcast.16, f32[32]{0:T(128)} %e_hbm.1), custom_call_target="tpu_custom_call" | custom-call | tf_op jit(solution)/shard_map/deflate/pallas_call | solution.py:257
  30.3 0.8 %copy.8 = f32[3,2,12,2048]{3,1,2,0:T(2,128)} copy(f32[3,2,12,2048]{3,1,2,0:T(2,128)S(1)} %bitcast.15) | data formatting | bytes 1179648

commit v5 on v4

--- a/solution.py
+++ b/solution.py
@@ -40,18 +40,6 @@
         peers.append((m, other, Y_ORDER[i]))
         if i < 7:
             peers.append((m, t, jnp.where(i < at, Y_ORDER[i], Y_ORDER[i + 1])))
-    return peers
-
-
-def line_peers():
-    m, t, g, near, far = places()
-    z, core = t // 2, lax.rem(t, 2)
-    peers = []
-    for i in range(8):
-        peers.append(((far, 2 * i + core, g), 2))
-        peers.append(((near, 2 * i + core, g), 1))
-        if i < 7:
-            peers.append(((m, 2 * jnp.where(i < z, i, i + 1) + core, g), 0))
     return peers
 
 
@@ -141,7 +129,7 @@
 def kernel(
     v_hbm, b_hbm, e_hbm, o_ref,
     v, b, e, tile, pick, spread, row_of, inverse, pair, first, slots1, second, slots2, send, recv,
-    load_sem, pair_send, pair_recv, send1, recv1, send2, recv2, send3, recv3,
+    load_sem, pair_send, pair_recv, send1, recv1, send2, recv2, send3, recv3, entered,
 ):
     m, t, g, near, far = places()
     core, z = lax.rem(t, 2), t // 2
@@ -152,23 +140,45 @@
     for copy in loads:
         copy.start()
 
-    plane, line = plane_peers(), line_peers()
+    plane = plane_peers()
     barrier = pltpu.get_barrier_semaphore()
-    for place in plane[::-1] + [p for p, _ in line]:
-        pl.semaphore_signal(barrier, inc=1, device_id=place, device_id_type=MESH)
+    beside = ((near, t, g), (far, t, g))
+    groups = ((far, 2), (near, 1), (m, 0))
+
+    def signal(sem, place):
+        pl.semaphore_signal(sem, inc=1, device_id=place, device_id_type=MESH)
+
+    def higher(act):
+        for i in range(7, 0, -1):
+            pl.when(i > z)(functools.partial(act, i))
+
+    def lower(act):
+        for i in range(7):
+            pl.when(i < z)(functools.partial(act, i))
+
+    def greet(i):
+        for mode, _ in groups:
+            signal(barrier, (mode, 2 * i + core, g))
+
+    def invite(i):
+        for mode, _ in groups:
+            signal(entered, (mode, 2 * i + core, g))
+
+    for place in plane[::-1] + list(beside):
+        signal(barrier, place)
+    higher(greet)
     tables1(tile, pick)
     loads[0].wait()
     loads[1].wait()
     mine = partial_coefs(v, b, tile, pick)
     first[...] = mine
-    pl.semaphore_wait(barrier, len(plane) + len(line))
+    pl.semaphore_wait(barrier, len(plane) + len(beside) + 3 * z)
 
     own = g * 2 + core
     for place in plane:
         pltpu.make_async_remote_copy(
             first, slots1.at[own], send1, recv1, device_id=place, device_id_type=MESH
         ).start()
-    beside = ((near, t, g), (far, t, g))
     exchange = []
     for h in range(2):
         copy = pltpu.make_async_remote_copy(
@@ -177,6 +187,7 @@
         )
         copy.start()
         exchange.append(copy)
+    lower(invite)
     slots1[own] = mine
     tables2(spread, row_of, (far, near, m))
     loads[2].wait()
@@ -191,12 +202,27 @@
     total = slots1[...].sum(axis=0)
 
     second[...] = total
-    for place, group in line:
+
+    def post(place, group):
         pltpu.make_async_remote_copy(
             second, slots2.at[group * 8 + z], send2, recv2, device_id=place, device_id_type=MESH
         ).start()
+
+    def post_all(i):
+        for mode, group in groups:
+            post((mode, 2 * i + core, g), group)
+
+    lower(post_all)
+    post(beside[1], 2)
+    post(beside[0], 1)
     slots2[z] = total
-    got2 = slots2.at[pl.ds(0, len(line))]
+
+    @pl.when(z < 7)
+    def _():
+        pl.semaphore_wait(entered, 3 * (7 - z))
+        higher(post_all)
+
+    got2 = slots2.at[pl.ds(0, 23)]
     pltpu.make_async_copy(got2, got2, recv2).wait()
     sums = [slots2[8 * i : 8 * i + 8].sum(axis=0) for i in range(3)]
 
@@ -280,6 +306,7 @@
             pltpu.VMEM((OUT, C, 2 * T, 128), BF16),
             pltpu.VMEM((OUT, C, 2 * T, 128), BF16),
             dma((3,)), dma((2,)), dma((2,)), dma, dma, dma, dma, dma((C // WIDTH,)), dma((C // WIDTH,)),
+            pltpu.SemaphoreType.REGULAR,
         ],
         compiler_params=pltpu.CompilerParams(
             collective_id=0, has_side_effects=True, vmem_limit_bytes=60 * 2**20

time: 31.3 us -> 29.3 us (0.936)
  the two profiles are of different devices: /device:TPU:1 before, /device:TPU:2 now
where the time goes in v5:
time: 29.3 us; the launch traced here: 29.2 us
  Pallas kernels  28.4 us (97%)
  local copies, waits for them, and re-layouts  0.82 us (3%)
    pallas_call x1, Pallas kernels, on_device(): pl.pallas_call(kernel, out_shape=pltpu.VMEM((OUT, C, 2 * T, 128), F32), i...  28.4 us
    unnamed x1, local copies, waits for them, and re-layouts  0.82 us

profile of v5, /device:TPU:2, one launch (start us, length us, event | category | flops | bytes accessed | tf_op | source)
XLA Modules:
  0.0 29.2 jit_solution(8125666260298750010)
XLA Ops:
  0.0 28.4 %deflate.1 = f32[3,12,32,128]{3,2,1,0:T(8,128)S(1)} custom-call(bf16[8,12,32,128]{3,2,1,0:T(8,128)(2,1)} %bitcast.17, bf16[12,12,32,128]{3,2,1,0:T(8,128)(2,1)} %bitcast.16, f32[32]{0:T(128)} %e_hbm.1), custom_call_target="tpu_custom_call" | custom-call | tf_op jit(solution)/shard_map/deflate/pallas_call | solution.py:283
  28.4 0.8 %copy.8 = f32[3,2,12,2048]{3,1,2,0:T(2,128)} copy(f32[3,2,12,2048]{3,1,2,0:T(2,128)S(1)} %bitcast.15) | data formatting | bytes 1179648

commit v6 on v5

--- a/solution.py
+++ b/solution.py
@@ -72,7 +72,8 @@
         blocks.append(y)
     y = split3(jnp.concatenate(blocks, axis=1))
     z = jnp.dot(y, pick[...], preferred_element_type=F32)
-    return z[0:8] + z[8:16] + z[16:24]
+    z = z[0:8] + z[8:16] + z[16:24]
+    return jnp.where(iota((4, 128), 1) < 64, z[0:4], pltpu.roll(z[4:8], 64, 1))
 
 
 def tables1(tile, pick):
@@ -224,7 +225,10 @@
 
     got2 = slots2.at[pl.ds(0, 23)]
     pltpu.make_async_copy(got2, got2, recv2).wait()
-    sums = [slots2[8 * i : 8 * i + 8].sum(axis=0) for i in range(3)]
+    sums = []
+    for i in range(3):
+        both = slots2[8 * i : 8 * i + 8].sum(axis=0)
+        sums.append(jnp.concatenate([both, pltpu.roll(both, 64, 1)], axis=0))
 
     blocks = coefs_of(sums, inverse)
     left = weights(blocks, row_of, ((0, (0, 1)), (1, (0, 2))), spread, tile)
@@ -299,10 +303,10 @@
             pltpu.VMEM((3 * OUT, 8, 128), F32),
             pltpu.VMEM((3, 8, 128), F32),
             pltpu.VMEM((2, K, HALF, 2 * T, 128), BF16),
-            pltpu.VMEM((8, 128), F32),
-            pltpu.VMEM((16, 8, 128), F32),
-            pltpu.VMEM((8, 128), F32),
-            pltpu.VMEM((24, 8, 128), F32),
+            pltpu.VMEM((4, 128), F32),
+            pltpu.VMEM((16, 4, 128), F32),
+            pltpu.VMEM((4, 128), F32),
+            pltpu.VMEM((24, 4, 128), F32),
             pltpu.VMEM((OUT, C, 2 * T, 128), BF16),
             pltpu.VMEM((OUT, C, 2 * T, 128), BF16),
             dma((3,)), dma((2,)), dma((2,)), dma, dma, dma, dma, dma((C // WIDTH,)), dma((C // WIDTH,)),

time: 29.3 us -> 29.3 us (level)
  no operation moved by 1% of the time
where the time goes in v6:
time: 29.3 us; the launch traced here: 29.1 us
  Pallas kernels  28.3 us (97%)
  local copies, waits for them, and re-layouts  0.82 us (3%)
    pallas_call x1, Pallas kernels, on_device(): pl.pallas_call(kernel, out_shape=pltpu.VMEM((OUT, C, 2 * T, 128), F32), i...  28.3 us
    unnamed x1, local copies, waits for them, and re-layouts  0.82 us

profile of v6, /device:TPU:2, one launch (start us, length us, event | category | flops | bytes accessed | tf_op | source)
XLA Modules:
  0.0 29.1 jit_solution(15285957000352332732)
XLA Ops:
  0.0 28.3 %deflate.1 = f32[3,12,32,128]{3,2,1,0:T(8,128)S(1)} custom-call(bf16[8,12,32,128]{3,2,1,0:T(8,128)(2,1)} %bitcast.17, bf16[12,12,32,128]{3,2,1,0:T(8,128)(2,1)} %bitcast.16, f32[32]{0:T(128)} %e_hbm.1), custom_call_target="tpu_custom_call" | custom-call | tf_op jit(solution)/shard_map/deflate/pallas_call | solution.py:287
  28.3 0.8 %copy.8 = f32[3,2,12,2048]{3,1,2,0:T(2,128)} copy(f32[3,2,12,2048]{3,1,2,0:T(2,128)S(1)} %bitcast.15) | data formatting | bytes 1179648
